TPU v7x, 512 devices: a whole 4x8x8 slice. The times are simulated.
512 devices in a mesh: band: 8 (over z_lo, core), row: 64 (over z_hi, x, y).
Axes of the slice: x: 4, y: 8, z: 8 (z_hi: 2, z_lo: 4; z = z_hi * 4 + z_lo), core: 2. Of those that a mesh axis runs over, the one named last changes fastest.
Arguments:
- latent: float32 [65536, 128], P(('band', 'row')), may hold values from -48 to 48
- input_proj: bfloat16 [2, 128, 1024], P(None, 'row'), may hold values from -0.5 to 0.5
- qkv_proj: bfloat16 [2, 1024, 1536], P(None, 'row'), may hold values from -4 to 4
- mix_proj: bfloat16 [2, 512, 1024], P(None, 'row'), may hold values from -0.25 to 0.25
- affine_head: bfloat16 [2, 1024, 256], P(None, 'row'), may hold values from -0.09375 to 0.09375
- attn_gain: float32 [2, 1024], replicated, may hold values from 0.5 to 1.5
- head_gain: float32 [2, 1024], replicated, may hold values from 0.5 to 1.5
Outputs:
- flow_out: float32 [65536, 128], P(('band', 'row'))
All inputs are finite; a program needn't handle non-finite values.
Results may differ from a plain program's by a relative error of at most 0.008.
Values may be sent and summed in bfloat16 or wider, within the bound.
A program may use at most 64 MiB of HBM per device.

v0:
```python
import math

import jax
import jax.numpy as jnp
from jax import lax
from jax.sharding import PartitionSpec as P

G = 256
HEADS = 4
HS = 128
WIN = 1024


EPS = 1e-06


def passed_along(x, axis, by):
    peers = lax.axis_size(axis)
    pairs = [(i, i + by) for i in range(peers) if 0 <= i + by < peers]
    return lax.ppermute(x, axis, pairs)


def normed(values, gains):
    inverse = lax.rsqrt(jnp.mean(values * values, axis=-1, keepdims=True) + EPS)
    return (values * inverse * gains).astype(jnp.bfloat16)


def contract(left, shard_rows):
    return jnp.dot(left, shard_rows, preferred_element_type=jnp.float32)


def contract_split(left, inner_width, shard_rows):
    query_sum = jnp.dot(left, shard_rows[:, :inner_width], preferred_element_type=jnp.float32)
    pair_sum = jnp.dot(left, shard_rows[:, inner_width:], preferred_element_type=jnp.float32)
    return (query_sum, pair_sum)


def attend(query_rows, window_keys, query_pos, key_pos):
    inner_width = HEADS * HS
    queries = query_rows.reshape(-1, HEADS, HS)
    key_part = window_keys[:, :inner_width].reshape(-1, HEADS, HS)
    value_part = window_keys[:, inner_width:].reshape(-1, HEADS, HS)
    scores = jnp.einsum("qhd,khd->hqk", queries, key_part, preferred_element_type=jnp.float32) * (
        1.0 / math.sqrt(HS)
    )
    allowed = (
        (key_pos[None, :] <= query_pos[:, None])
        & (key_pos[None, :] > query_pos[:, None] - WIN)
        & (key_pos[None, :] >= 0)
    )
    scores = jnp.where(allowed[None], scores, -1e30)
    highest = jnp.max(scores, axis=-1, keepdims=True)
    weights = jnp.exp(scores - highest)
    probs = (weights / jnp.sum(weights, axis=-1, keepdims=True)).astype(jnp.bfloat16)
    result = jnp.einsum("hqk,khd->qhd", probs, value_part, preferred_element_type=jnp.float32)
    return result.reshape(-1, inner_width).astype(jnp.bfloat16)


def window_attention(queries, key_rows, first_pos):
    tokens = queries.shape[0]
    block_rows = min(tokens, 512)
    block_count = tokens // block_rows
    grouped = queries.reshape(block_count, block_rows, queries.shape[1])

    def one_block(packed):
        query_rows, block_index = packed
        offset = block_index * block_rows
        query_pos = first_pos + offset + jnp.arange(block_rows, dtype=jnp.int32)
        key_pos = first_pos + offset - WIN + jnp.arange(WIN + block_rows, dtype=jnp.int32)
        return attend(query_rows, key_rows, query_pos, key_pos)

    result = lax.map(one_block, (grouped, jnp.arange(block_count, dtype=jnp.int32)))
    return result.reshape(tokens, queries.shape[1])


def flow_block(flow_state, w_in, w_qkv, w_mix, w_head, gain_attn, gain_head):
    tokens, channels = flow_state.shape
    inner_width = HEADS * HS
    first_pos = lax.axis_index(("band", "row")) * tokens
    reach_back = -(-WIN // tokens)
    rounded = flow_state.astype(jnp.bfloat16)
    hidden = contract(rounded, lax.all_gather(w_in, "row", axis=0, tiled=True))
    normed_in = normed(hidden, gain_attn)
    query_sum, pair_sum = contract_split(
        normed_in, inner_width, lax.all_gather(w_qkv, "row", axis=0, tiled=True)
    )
    queries = query_sum.astype(jnp.bfloat16)
    own_pairs = pair_sum.astype(jnp.bfloat16)
    earlier = [
        passed_along(own_pairs, ("band", "row"), distance) for distance in range(reach_back, 0, -1)
    ]
    key_rows = jnp.concatenate(earlier + [own_pairs], axis=0)
    attended = window_attention(queries, key_rows, first_pos)
    hidden = hidden + contract(attended, lax.all_gather(w_mix, "row", axis=0, tiled=True))
    normed_out = normed(hidden, gain_head)
    params = contract(normed_out, lax.all_gather(w_head, "row", axis=0, tiled=True))
    final_row = passed_along(params[tokens - 1 :], ("band", "row"), 1)
    shifted = jnp.concatenate([final_row, params[:-1]], axis=0)
    return (flow_state - shifted[:, :channels]) * jnp.exp(-shifted[:, channels:])


def transpose_grid(flow_state):
    tokens, channels = flow_state.shape
    band_count = lax.axis_size("band")
    row_count = lax.axis_size("row")
    device = lax.axis_index(("band", "row"))
    pieces_per_row = G // tokens
    pair_slots = 1
    choose_col = (jnp.arange(pieces_per_row, dtype=jnp.int32) == device % pieces_per_row).astype(
        jnp.float32
    )
    choose_half = (
        jnp.arange(pieces_per_row, dtype=jnp.int32) == device // pieces_per_row // tokens
    ).astype(jnp.float32)
    outgoing = (
        flow_state[None, :, None, :]
        * choose_col[:, None, None, None]
        * choose_half[None, None, :, None]
    )
    outgoing = outgoing.reshape(band_count, row_count, pair_slots, channels)
    incoming = lax.all_to_all(
        lax.all_to_all(
            outgoing.astype(jnp.bfloat16), "band", split_axis=0, concat_axis=0, tiled=True
        ),
        "row",
        split_axis=1,
        concat_axis=1,
        tiled=True,
    ).astype(outgoing.dtype)
    arranged = incoming.reshape(G, pieces_per_row, channels)
    column = device // pieces_per_row
    picked = lax.dynamic_slice_in_dim(arranged, device % pieces_per_row * tokens, tokens, 0)
    picked = lax.dynamic_slice_in_dim(picked, column // tokens, 1, 1)
    return picked.reshape(tokens, channels)


def shards(latent, input_proj, qkv_proj, mix_proj, affine_head, attn_gain, head_gain):
    flow_state = latent
    for section_index in range(input_proj.shape[0]):
        if section_index > 0:
            flow_state = transpose_grid(flow_state)
        flow_state = flow_block(
            flow_state,
            input_proj[section_index],
            qkv_proj[section_index],
            mix_proj[section_index],
            affine_head[section_index],
            attn_gain[section_index],
            head_gain[section_index],
        )
    return flow_state


def solution(mesh):
    return jax.shard_map(
        shards,
        mesh=mesh,
        in_specs=(
            P(("band", "row"), None),
            P(None, "row", None),
            P(None, "row", None),
            P(None, "row", None),
            P(None, "row", None),
            P(),
            P(),
        ),
        out_specs=P(("band", "row"), None),
        check_vma=False,
    )
```

profile of v0, /device:TPU:1, one launch (start us, length us, event | category | flops | bytes accessed | tf_op | source)
XLA Modules:
  0.0 1178.7 jit_solution(892167972950251390)
XLA Ops:
  6.5 1.4 fusion.84
  11.5 204.4 %all-gather = bf16[1,128,1024]{2,0,1:T(2,128)(2,1)S(1)} all-gather(bf16[1,2,1024]{2,0,1:T(2,128)(2,1)S(1)} %copy.44), channel_id=2, replica_groups=mesh['band'=8,'row'=64] {'row'}, dimensions={1}, use_global_device_ids=true | all-gather | bytes 266240 | tf_op jit(solution)/shard_map/all_gather | solution.py:82
  217.1 1.4 fusion.88
  218.5 1.4 fusion.87
  221.2 188.8 %all-gather.3 = bf16[1,1024,256]{2,1,0:T(8,128)(2,1)S(1)} all-gather(bf16[1,16,256]{2,1,0:T(8,128)(2,1)S(1)} %get-tuple-element.44), channel_id=5, replica_groups=mesh['band'=8,'row'=64] {'row'}, dimensions={1}, use_global_device_ids=true | all-gather | bytes 532480 | tf_op jit(solution)/shard_map/all_gather | solution.py:96
  410.2 2.1 fusion.12
  412.4 1.9 collective-permute-start
  414.8 1.9 collective-permute-start.1
  416.7 1.9 collective-permute-start.2
  418.7 1.9 collective-permute-start.3
  420.6 1.9 collective-permute-start.4
  422.5 2.3 fusion.26
  424.8 26.5 %collective-permute-done = bf16[128,1024]{1,0:T(8,128)(2,1)S(1)} collective-permute-done((bf16[128,1024]{1,0:T(8,128)(2,1)S(1)}, bf16[128,1024]{1,0:T(8,128)(2,1)S(1)}, u32[]{:S(2)}, u32[]{:S(2)}) %collective-permute-start) | collective-permute-done | bytes 262176 | tf_op jit(solution)/shard_map/ppermute | solution.py:20
  451.3 12.6 %collective-permute-start.5 = (bf16[128,1024]{1,0:T(8,128)(2,1)S(1)}, bf16[128,1024]{1,0:T(8,128)(2,1)S(1)}, u32[]{:S(2)}, u32[]{:S(2)}) collective-permute-start(bf16[128,1024]{1,0:T(8,128)(2,1)S(1)} %fusion.12), channel_id=1, source_target_pairs={{0,3},{1,4},{2,5},{3,6},{4,7},{5,8},{6,9},{7,10},{8,11},{9,12},{10... | collective-permute-start | bytes 786440 | tf_op jit(solution)/shard_map/ppermute | solution.py:20
  464.0 15.4 %collective-permute-start.6 = (bf16[128,1024]{1,0:T(8,128)(2,1)S(1)}, bf16[128,1024]{1,0:T(8,128)(2,1)S(1)}, u32[]{:S(2)}, u32[]{:S(2)}) collective-permute-start(bf16[128,1024]{1,0:T(8,128)(2,1)S(1)} %fusion.12), channel_id=1, source_target_pairs={{0,2},{1,3},{2,4},{3,5},{4,6},{5,7},{6,8},{7,9},{8,10},{9,11},{10,... | collective-permute-start | bytes 786440 | tf_op jit(solution)/shard_map/ppermute | solution.py:20
  479.4 8.6 collective-permute-start.7
  488.1 21.8 %collective-permute-done.6 = bf16[128,1024]{1,0:T(8,128)(2,1)S(1)} collective-permute-done((bf16[128,1024]{1,0:T(8,128)(2,1)S(1)}, bf16[128,1024]{1,0:T(8,128)(2,1)S(1)}, u32[]{:S(2)}, u32[]{:S(2)}) %collective-permute-start.6) | collective-permute-done | bytes 262176 | tf_op jit(solution)/shard_map/ppermute | solution.py:20
  510.0 7.8 collective-permute-done.7
  519.9 3.7 fusion.90
  523.7 2.3 fusion.25
  526.0 1.6 multiply_reduce_fusion.2
  528.0 9.7 collective-permute-start.8
  537.9 6.0 collective-permute-done.8
  544.2 65.8 %all_to_all.10 = bf16[8,64,1,128]{3,1,2,0:T(8,128)(2,1)S(1)} all-to-all(bf16[8,64,1,128]{3,1,2,0:T(8,128)(2,1)S(1)} %multiply_convert_fusion.6), channel_id=1, replica_groups=mesh['band'=8,'row'=64] {'band'}, dimensions={0} | all-to-all | bytes 262144 | tf_op jit(solution)/shard_map/all_to_all | solution.py:122
  610.7 7.2 all-to-all-start.1
  618.5 197.7 %all-gather.4 = bf16[1,128,1024]{2,0,1:T(2,128)(2,1)S(1)} all-gather(bf16[1,2,1024]{2,0,1:T(2,128)(2,1)S(1)} %copy.45), channel_id=6, replica_groups=mesh['band'=8,'row'=64] {'row'}, dimensions={1}, use_global_device_ids=true | all-gather | bytes 266240 | tf_op jit(solution)/shard_map/all_gather | solution.py:82
  816.7 2.1 fusion.15
  818.8 1.9 collective-permute-start.9
  820.7 193.4 %all-gather.7 = bf16[1,1024,256]{2,1,0:T(8,128)(2,1)S(1)} all-gather(bf16[1,16,256]{2,1,0:T(8,128)(2,1)S(1)} %copy-done.2), channel_id=9, replica_groups=mesh['band'=8,'row'=64] {'row'}, dimensions={1}, use_global_device_ids=true | all-gather | bytes 532480 | tf_op jit(solution)/shard_map/all_gather | solution.py:96
  1014.1 1.9 collective-permute-start.10
  1016.0 1.9 collective-permute-start.11
  1017.9 2.2 fusion.27
  1020.2 1.9 collective-permute-start.12
  1022.1 1.9 collective-permute-start.13
  1024.0 1.9 collective-permute-start.14
  1026.0 25.2 %collective-permute-done.10 = bf16[128,1024]{1,0:T(8,128)(2,1)S(1)} collective-permute-done((bf16[128,1024]{1,0:T(8,128)(2,1)S(1)}, bf16[128,1024]{1,0:T(8,128)(2,1)S(1)}, u32[]{:S(2)}, u32[]{:S(2)}) %collective-permute-start.10) | collective-permute-done | bytes 262176 | tf_op jit(solution)/shard_map/ppermute | solution.py:20
  1051.2 9.3 collective-permute-start.15
  1060.5 5.3 collective-permute-done.11
  1065.9 6.6 collective-permute-start.16
  1072.5 4.4 collective-permute-done.13
  1076.9 4.8 collective-permute-done.14
  1081.7 40.4 %collective-permute-done.15 = bf16[128,1024]{1,0:T(8,128)(2,1)S(1)} collective-permute-done((bf16[128,1024]{1,0:T(8,128)(2,1)S(1)}, bf16[128,1024]{1,0:T(8,128)(2,1)S(1)}, u32[]{:S(2)}, u32[]{:S(2)}) %collective-permute-start.15) | collective-permute-done | bytes 262176 | tf_op jit(solution)/shard_map/ppermute | solution.py:20
  1122.1 26.3 %collective-permute-done.16 = bf16[128,1024]{1,0:T(8,128)(2,1)S(1)} collective-permute-done((bf16[128,1024]{1,0:T(8,128)(2,1)S(1)}, bf16[128,1024]{1,0:T(8,128)(2,1)S(1)}, u32[]{:S(2)}, u32[]{:S(2)}) %collective-permute-start.16) | collective-permute-done | bytes 262176 | tf_op jit(solution)/shard_map/ppermute | solution.py:20
  1150.5 3.7 fusion.95
  1154.2 2.3 fusion.24
  1156.5 1.6 multiply_reduce_fusion
  1158.5 1.9 collective-permute-start.17
  1160.4 11.1 collective-permute-done.17
  (89 shorter events, 14.7 us)
Async XLA Ops:
  6.5 403.7 %all-gather.13.cloned.1.call-start = ((), (), s32[]{:S(2)}) async-start(), calls=%async_computation.2 | async-start | bytes 3194880 | tf_op jit(solution)/shard_map/all_gather | solution.py:85
  8.0 518.0 %all-gather.15.cloned.1.call-start = ((), (), s32[]{:S(2)}) async-start(), calls=%async_computation.3 | async-start | bytes 1064960 | tf_op jit(solution)/shard_map/all_gather | solution.py:94
  9.4 807.2 %all-gather.17.cloned.1.call-start = ((), (), s32[]{:S(2)}) async-start(), calls=%async_computation.4 | async-start | bytes 3194880 | tf_op jit(solution)/shard_map/all_gather | solution.py:85
  410.2 109.7 %copy-start.1 = (pred[128,1152]{1,0:T(8,128)(4,1)}, pred[128,1152]{1,0:T(8,128)(4,1)S(1)}, u32[]{:S(2)}) copy-start(pred[128,1152]{1,0:T(8,128)(4,1)S(1)} %and_and_fusion) | copy-start | bytes 442372
  412.4 39.0 %collective-permute-start = (bf16[128,1024]{1,0:T(8,128)(2,1)S(1)}, bf16[128,1024]{1,0:T(8,128)(2,1)S(1)}, u32[]{:S(2)}, u32[]{:S(2)}) collective-permute-start(bf16[128,1024]{1,0:T(8,128)(2,1)S(1)} %fusion.12), channel_id=1, source_target_pairs={{0,8},{1,9},{2,10},{3,11},{4,12},{5,13},{6,14},{7,15},{8,16},{9,17... | collective-permute-start | bytes 786440 | tf_op jit(solution)/shard_map/ppermute | solution.py:20
  414.8 49.1 %collective-permute-start.1 = (bf16[128,1024]{1,0:T(8,128)(2,1)S(1)}, bf16[128,1024]{1,0:T(8,128)(2,1)S(1)}, u32[]{:S(2)}, u32[]{:S(2)}) collective-permute-start(bf16[128,1024]{1,0:T(8,128)(2,1)S(1)} %fusion.12), channel_id=1, source_target_pairs={{0,7},{1,8},{2,9},{3,10},{4,11},{5,12},{6,13},{7,14},{8,15},{9,16}... | collective-permute-start | bytes 786440 | tf_op jit(solution)/shard_map/ppermute | solution.py:20
  416.7 62.6 %collective-permute-start.2 = (bf16[128,1024]{1,0:T(8,128)(2,1)S(1)}, bf16[128,1024]{1,0:T(8,128)(2,1)S(1)}, u32[]{:S(2)}, u32[]{:S(2)}) collective-permute-start(bf16[128,1024]{1,0:T(8,128)(2,1)S(1)} %fusion.12), channel_id=1, source_target_pairs={{0,6},{1,7},{2,8},{3,9},{4,10},{5,11},{6,12},{7,13},{8,14},{9,15},... | collective-permute-start | bytes 786440 | tf_op jit(solution)/shard_map/ppermute | solution.py:20
  418.7 69.4 %collective-permute-start.3 = (bf16[128,1024]{1,0:T(8,128)(2,1)S(1)}, bf16[128,1024]{1,0:T(8,128)(2,1)S(1)}, u32[]{:S(2)}, u32[]{:S(2)}) collective-permute-start(bf16[128,1024]{1,0:T(8,128)(2,1)S(1)} %fusion.12), channel_id=1, source_target_pairs={{0,5},{1,6},{2,7},{3,8},{4,9},{5,10},{6,11},{7,12},{8,13},{9,14},{... | collective-permute-start | bytes 786440 | tf_op jit(solution)/shard_map/ppermute | solution.py:20
  420.6 67.5 %collective-permute-start.4 = (bf16[128,1024]{1,0:T(8,128)(2,1)S(1)}, bf16[128,1024]{1,0:T(8,128)(2,1)S(1)}, u32[]{:S(2)}, u32[]{:S(2)}) collective-permute-start(bf16[128,1024]{1,0:T(8,128)(2,1)S(1)} %fusion.12), channel_id=1, source_target_pairs={{0,4},{1,5},{2,6},{3,7},{4,8},{5,9},{6,10},{7,11},{8,12},{9,13},{1... | collective-permute-start | bytes 786440 | tf_op jit(solution)/shard_map/ppermute | solution.py:20
  451.3 36.8 %collective-permute-start.5 = (bf16[128,1024]{1,0:T(8,128)(2,1)S(1)}, bf16[128,1024]{1,0:T(8,128)(2,1)S(1)}, u32[]{:S(2)}, u32[]{:S(2)}) collective-permute-start(bf16[128,1024]{1,0:T(8,128)(2,1)S(1)} %fusion.12), channel_id=1, source_target_pairs={{0,3},{1,4},{2,5},{3,6},{4,7},{5,8},{6,9},{7,10},{8,11},{9,12},{10... | collective-permute-start | bytes 786440 | tf_op jit(solution)/shard_map/ppermute | solution.py:20
  464.0 46.0 %collective-permute-start.6 = (bf16[128,1024]{1,0:T(8,128)(2,1)S(1)}, bf16[128,1024]{1,0:T(8,128)(2,1)S(1)}, u32[]{:S(2)}, u32[]{:S(2)}) collective-permute-start(bf16[128,1024]{1,0:T(8,128)(2,1)S(1)} %fusion.12), channel_id=1, source_target_pairs={{0,2},{1,3},{2,4},{3,5},{4,6},{5,7},{6,8},{7,9},{8,10},{9,11},{10,... | collective-permute-start | bytes 786440 | tf_op jit(solution)/shard_map/ppermute | solution.py:20
  479.4 38.4 %collective-permute-start.7 = (bf16[128,1024]{1,0:T(8,128)(2,1)S(1)}, bf16[128,1024]{1,0:T(8,128)(2,1)S(1)}, u32[]{:S(2)}, u32[]{:S(2)}) collective-permute-start(bf16[128,1024]{1,0:T(8,128)(2,1)S(1)} %fusion.12), channel_id=1, source_target_pairs={{0,1},{1,2},{2,3},{3,4},{4,5},{5,6},{6,7},{7,8},{8,9},{9,10},{10,1... | collective-permute-start | bytes 786440 | tf_op jit(solution)/shard_map/ppermute | solution.py:20
  523.7 4.0 copy-start.4
  525.9 17.9 %copy-start = (f32[128,128]{1,0:T(8,128)S(1)}, f32[128,128]{1,0:T(8,128)}, u32[]{:S(2)}) copy-start(f32[128,128]{1,0:T(8,128)} %param.7) | copy-start | bytes 196612
  525.9 17.9 %copy-start.7 = (f32[2]{0:T(128)S(1)}, f32[2]{0:T(128)}, u32[]{:S(2)}) copy-start(f32[2]{0:T(128)} %compare_convert_fusion.1) | copy-start | bytes 28
  526.0 92.5 %copy-start.5 = (bf16[1,2,1024]{2,1,0:T(2,128)(2,1)S(1)}, bf16[1,2,1024]{2,1,0:T(2,128)(2,1)}, u32[]{:S(2)}) copy-start(bf16[1,2,1024]{2,1,0:T(2,128)(2,1)} %get-tuple-element.49) | copy-start | bytes 12292
  528.0 288.7 %copy-start.6 = (f32[1,1024]{1,0:T(1,128)S(1)}, f32[1,1024]{1,0:T(1,128)}, u32[]{:S(2)}) copy-start(f32[1,1024]{1,0:T(1,128)} %get-tuple-element.47) | copy-start | bytes 12292
  528.0 15.9 %collective-permute-start.8 = (f32[1,256]{1,0:T(1,128)S(1)}, f32[1,256]{1,0:T(1,128)S(1)}, u32[]{:S(2)}, u32[]{:S(2)}) collective-permute-start(f32[1,256]{1,0:T(1,128)S(1)} %slice.120), channel_id=1, source_target_pairs={{0,1},{1,2},{2,3},{3,4},{4,5},{5,6},{6,7},{7,8},{8,9},{9,10},{10,1... | collective-permute-start | bytes 3080 | tf_op jit(solution)/shard_map/ppermute | solution.py:20
  610.7 205.5 %all-to-all-start.1 = ((bf16[8,64,1,128]{3,0,2,1:T(8,128)(2,1)}), bf16[8,64,1,128]{3,0,2,1:T(8,128)(2,1)S(1)}, u32[]{:S(2)}, u32[]{:S(2)}) async-start(bf16[8,64,1,128]{3,0,2,1:T(8,128)(2,1)} %copy.34), calls=%async_computation.1 | async-start | bytes 262144 | tf_op jit(solution)/shard_map/all_to_all | solution.py:121
  617.9 538.6 %all-gather.19.cloned.1.call-start = ((), (), s32[]{:S(2)}) async-start(), calls=%async_computation.5 | async-start | bytes 1064960 | tf_op jit(solution)/shard_map/all_gather | solution.py:94
  816.2 4.5 copy-start.2
  818.8 205.3 %collective-permute-start.9 = (bf16[128,1024]{1,0:T(8,128)(2,1)S(1)}, bf16[128,1024]{1,0:T(8,128)(2,1)S(1)}, u32[]{:S(2)}, u32[]{:S(2)}) collective-permute-start(bf16[128,1024]{1,0:T(8,128)(2,1)S(1)} %fusion.15), channel_id=1, source_target_pairs={{0,8},{1,9},{2,10},{3,11},{4,12},{5,13},{6,14},{7,15},{8,16},{9,17... | collective-permute-start | bytes 786440 | tf_op jit(solution)/shard_map/ppermute | solution.py:20
  1014.1 37.1 %collective-permute-start.10 = (bf16[128,1024]{1,0:T(8,128)(2,1)S(1)}, bf16[128,1024]{1,0:T(8,128)(2,1)S(1)}, u32[]{:S(2)}, u32[]{:S(2)}) collective-permute-start(bf16[128,1024]{1,0:T(8,128)(2,1)S(1)} %fusion.15), channel_id=1, source_target_pairs={{0,7},{1,8},{2,9},{3,10},{4,11},{5,12},{6,13},{7,14},{8,15},{9,16}... | collective-permute-start | bytes 786440 | tf_op jit(solution)/shard_map/ppermute | solution.py:20
  1016.0 49.9 %collective-permute-start.11 = (bf16[128,1024]{1,0:T(8,128)(2,1)S(1)}, bf16[128,1024]{1,0:T(8,128)(2,1)S(1)}, u32[]{:S(2)}, u32[]{:S(2)}) collective-permute-start(bf16[128,1024]{1,0:T(8,128)(2,1)S(1)} %fusion.15), channel_id=1, source_target_pairs={{0,6},{1,7},{2,8},{3,9},{4,10},{5,11},{6,12},{7,13},{8,14},{9,15},... | collective-permute-start | bytes 786440 | tf_op jit(solution)/shard_map/ppermute | solution.py:20
  1020.2 52.3 %collective-permute-start.12 = (bf16[128,1024]{1,0:T(8,128)(2,1)S(1)}, bf16[128,1024]{1,0:T(8,128)(2,1)S(1)}, u32[]{:S(2)}, u32[]{:S(2)}) collective-permute-start(bf16[128,1024]{1,0:T(8,128)(2,1)S(1)} %fusion.15), channel_id=1, source_target_pairs={{0,5},{1,6},{2,7},{3,8},{4,9},{5,10},{6,11},{7,12},{8,13},{9,14},{... | collective-permute-start | bytes 786440 | tf_op jit(solution)/shard_map/ppermute | solution.py:20
  1022.1 54.8 %collective-permute-start.13 = (bf16[128,1024]{1,0:T(8,128)(2,1)S(1)}, bf16[128,1024]{1,0:T(8,128)(2,1)S(1)}, u32[]{:S(2)}, u32[]{:S(2)}) collective-permute-start(bf16[128,1024]{1,0:T(8,128)(2,1)S(1)} %fusion.15), channel_id=1, source_target_pairs={{0,4},{1,5},{2,6},{3,7},{4,8},{5,9},{6,10},{7,11},{8,12},{9,13},{1... | collective-permute-start | bytes 786440 | tf_op jit(solution)/shard_map/ppermute | solution.py:20
  1024.0 57.6 %collective-permute-start.14 = (bf16[128,1024]{1,0:T(8,128)(2,1)S(1)}, bf16[128,1024]{1,0:T(8,128)(2,1)S(1)}, u32[]{:S(2)}, u32[]{:S(2)}) collective-permute-start(bf16[128,1024]{1,0:T(8,128)(2,1)S(1)} %fusion.15), channel_id=1, source_target_pairs={{0,3},{1,4},{2,5},{3,6},{4,7},{5,8},{6,9},{7,10},{8,11},{9,12},{10... | collective-permute-start | bytes 786440 | tf_op jit(solution)/shard_map/ppermute | solution.py:20
  1051.2 70.9 %collective-permute-start.15 = (bf16[128,1024]{1,0:T(8,128)(2,1)S(1)}, bf16[128,1024]{1,0:T(8,128)(2,1)S(1)}, u32[]{:S(2)}, u32[]{:S(2)}) collective-permute-start(bf16[128,1024]{1,0:T(8,128)(2,1)S(1)} %fusion.15), channel_id=1, source_target_pairs={{0,2},{1,3},{2,4},{3,5},{4,6},{5,7},{6,8},{7,9},{8,10},{9,11},{10,... | collective-permute-start | bytes 786440 | tf_op jit(solution)/shard_map/ppermute | solution.py:20
  1065.9 82.6 %collective-permute-start.16 = (bf16[128,1024]{1,0:T(8,128)(2,1)S(1)}, bf16[128,1024]{1,0:T(8,128)(2,1)S(1)}, u32[]{:S(2)}, u32[]{:S(2)}) collective-permute-start(bf16[128,1024]{1,0:T(8,128)(2,1)S(1)} %fusion.15), channel_id=1, source_target_pairs={{0,1},{1,2},{2,3},{3,4},{4,5},{5,6},{6,7},{7,8},{8,9},{9,10},{10,1... | collective-permute-start | bytes 786440 | tf_op jit(solution)/shard_map/ppermute | solution.py:20
  1154.2 3.9 copy-start.3
  1158.5 13.0 %collective-permute-start.17 = (f32[1,256]{1,0:T(1,128)S(1)}, f32[1,256]{1,0:T(1,128)S(1)}, u32[]{:S(2)}, u32[]{:S(2)}) collective-permute-start(f32[1,256]{1,0:T(1,128)S(1)} %slice.128), channel_id=1, source_target_pairs={{0,1},{1,2},{2,3},{3,4},{4,5},{5,6},{6,7},{7,8},{8,9},{9,10},{10,1... | collective-permute-start | bytes 3080 | tf_op jit(solution)/shard_map/ppermute | solution.py:20
Sparse Core Ops, SparseCore 0:
  11.8 149.9 all-gather.12
  166.3 122.6 all-gather.14
  293.5 151.3 all-gather.16
  622.9 127.2 all-gather.18
where the time goes:
time: 1190 us; the launch traced here: 1180 us
  blocking collectives  850 us (71%)
  waiting for transfers between devices  181 us (15%)
  starting transfers between devices  92.5 us (8%)
  matrix products  26 us (2%)
  between operations  13.8 us (1%)
  local copies, waits for them, and re-layouts  13.6 us (1%)
    all_gather x2, blocking collectives, flow_block(): hidden = contract(rounded, lax.all_gather(w_in, 'row', axis=0, tiled=True))  402 us
    all_gather x2, blocking collectives, flow_block(): lax.all_gather(w_head, 'row', axis=0, tiled=True)  382 us
    ppermute x18, waiting for transfers between devices, passed_along(): return lax.ppermute(x, axis, pairs)  180 us
    ppermute x18, starting transfers between devices, passed_along(): return lax.ppermute(x, axis, pairs)  85.2 us
    all_to_all x1, blocking collectives, transpose_grid(): lax.all_to_all(outgoing.astype(jnp.bfloat16), 'band', split_axis=0, conca...  65.8 us
  transfers between devices with their start and end apart: 23, of which 11 were waited for; matrix products, arithmetic and copies ran while one was open for 3% of the time, Pallas kernels for 0%

commit v1 on v0

v1 whole, which is shorter than its diff:
```python
import math

import jax
import jax.numpy as jnp
from jax import lax
from jax.experimental import pallas as pl
from jax.experimental.pallas import tpu as pltpu
from jax.sharding import PartitionSpec as P

MESH = pl.DeviceIdType.MESH
F32, BF16 = jnp.float32, jnp.bfloat16
G, C, D, HEADS, HS, WIN = 256, 128, 1024, 4, 128, 1024
INNER = HEADS * HS
TOK = 128
DEVICES = 512
NA = INNER + INNER + 256
NB = 128 + 2 * INNER
EXTRA = 16
ROWS = EXTRA + TOK
T0 = WIN + TOK
T1 = 5 * G
EPS = 1e-06
SCALE = math.log2(math.e) / math.sqrt(HS)


def place():
    band, row = lax.axis_index("band"), lax.axis_index("row")
    return band, row, band // 2, band % 2, row // 32, (row // 8) % 4, row % 8


def at_device(index):
    return (index // 64, index % 64)


class Gather:
    def __init__(self, wa, wb, sems):
        self.wa, self.wb, self.s = wa, wb, sems
        self.band, self.row, self.zlo, self.core, self.zhi, self.x, self.y = place()
        self.sent = ({}, {})

    def at(self, x=None, y=None, zhi=None, core=None):
        x = self.x if x is None else x
        y = self.y if y is None else y
        zhi = self.zhi if zhi is None else zhi
        core = self.core if core is None else core
        return (self.zlo * 2 + core, zhi * 32 + x * 8 + y)

    def copy(self, ref, sem, where):
        name, *index = sem
        return pltpu.make_async_remote_copy(
            src_ref=ref,
            dst_ref=ref,
            send_sem=self.s[name][0].at[*index],
            recv_sem=self.s[name][1].at[*index],
            device_id=where,
            device_id_type=MESH,
        )

    def send(self, core, ref, sem, where):
        self.copy(ref, sem, where).start()
        kind = "half" if sem[0] == "side" else "column" if len(ref.shape) == 3 else "cell" if ref.shape[0] == 16 else "line"
        self.sent[core][sem] = kind

    def got(self, ref, sem):
        self.copy(ref, sem, self.at()).wait_recv()

    def half(self, h):
        return self.zhi if h == 0 else 1 - self.zhi

    def cell(self, w, b, h, x, y):
        return w.at[b, 4 * self.half(h) + x, pl.ds(pl.multiple_of(16 * y, 16), 16)]

    def column(self, w, b, h, y):
        return w.at[b, pl.ds(4 * self.half(h), 4), pl.ds(pl.multiple_of(16 * y, 16), 16)]

    def line(self, w, b, h, x):
        return w.at[b, 4 * self.half(h) + x]

    def across(self, core, b):
        w = (self.wa, self.wb)[core]
        self.send(core, self.cell(w, b, 0, self.x, self.y), ("z", b), self.at(zhi=1 - self.zhi))

    def across_got(self, core, b):
        w = (self.wa, self.wb)[core]
        self.got(self.cell(w, b, 1, self.x, self.y), ("z", b))

    def a_x(self, b, h):
        for d in (1, 3, 2):
            self.send(0, self.cell(self.wa, b, h, self.x, self.y), ("ax", b, h, d), self.at(x=(self.x + d) % 4))

    def a_side(self, b, h, y):
        self.send(0, self.column(self.wa, b, h, y), ("side", b, h), self.at(core=1))

    def a_y(self, b, h, k):
        last = (4, 3) if h == 0 else (3, 4)
        if k == 0:
            for d in (1, 3, 2):
                self.got(self.cell(self.wa, b, h, (self.x - d) % 4, self.y), ("ax", b, h, d))
        for way, step in ((0, 1), (1, -1)):
            if k > last[way]:
                continue
            y = (self.y - step * k) % 8
            ref = self.column(self.wa, b, h, y)
            if k > 0:
                self.got(ref, ("ay", b, h, way, k))
            if k < last[way]:
                self.send(0, ref, ("ay", b, h, way, k + 1), self.at(y=(self.y + step) % 8))
            if k > 0 or way == 0:
                self.a_side(b, h, y)

    def b_y(self, b, h):
        for d in (4, 3, 5, 2, 6, 1, 7):
            self.send(1, self.cell(self.wb, b, h, self.x, self.y), ("by", b, h, d), self.at(y=(self.y + d) % 8))

    def b_x(self, b, h):
        for d in range(1, 8):
            self.got(self.cell(self.wb, b, h, self.x, (self.y - d) % 8), ("by", b, h, d))
        for d in (2, 1, 3):
            self.send(1, self.line(self.wb, b, h, self.x), ("bx", b, h, d), self.at(x=(self.x + d) % 4))
        self.b_side(b, h, self.x)

    def b_side(self, b, h, x):
        self.send(1, self.line(self.wb, b, h, x), ("side", b, h), self.at(core=0))

    def b_on(self, b, h, d):
        x = (self.x - d) % 4
        self.got(self.line(self.wb, b, h, x), ("bx", b, h, d))
        self.b_side(b, h, x)

    def side_got(self, core, b):
        w = (self.wb, self.wa)[core]
        for h in range(2):
            self.got(w.at[b, pl.ds(4 * self.half(h), 4)], ("side", b, h))

    def steps(self, core, b):
        if core == 0:
            yield lambda: self.across(0, b)
            yield lambda: self.a_x(b, 0)
            yield lambda: (self.across_got(0, b), self.a_x(b, 1))
            for k in range(5):
                yield lambda k=k: (self.a_y(b, 0, k), self.a_y(b, 1, k))
        else:
            yield lambda: self.across(1, b)
            yield lambda: self.b_y(b, 0)
            yield lambda: (self.across_got(1, b), self.b_y(b, 1))
            yield lambda: self.b_x(b, 0)
            yield lambda: self.b_x(b, 1)
            yield lambda: (self.b_on(b, 0, 1), self.b_on(b, 0, 3), self.b_on(b, 0, 2))
            yield lambda: (self.b_on(b, 1, 1), self.b_on(b, 1, 3), self.b_on(b, 1, 2))
            yield lambda: None
        yield lambda: self.side_got(core, b)

    def run(self, pairs):
        for first, second in pairs:
            pl.when(self.core == 0)(lambda: (first(), None)[1])
            pl.when(self.core == 1)(lambda: (second(), None)[1])

    def finish(self):
        for core in range(2):

            @pl.when(self.core == core)
            def _():
                w = (self.wa, self.wb)[core]
                whole = dict(
                    cell=w.at[0, 0, pl.ds(0, 16)],
                    column=w.at[0, pl.ds(0, 4), pl.ds(0, 16)],
                    line=w.at[0, 0],
                    half=w.at[0, pl.ds(0, 4)],
                )
                for sem, kind in self.sent[core].items():
                    self.copy(whole[kind], sem, self.at()).wait_send()


def inverse_rms(values):
    return lax.rsqrt(jnp.mean(values * values, axis=-1, keepdims=True) + EPS)


def kernel(
    latent, w_in, w_qkv, w_mix, w_head, gain_attn, gain_head, out,
    wa, wb, win, wmix, unpack, halo, tile_a, tile_b, grid_rows, natural, query_state,
    normed, pairs, attended, params, state,
    zsem, zsend, axsem, axsend, aysem, aysend, bysem, bysend, bxsem, bxsend, side, side_send,
    hsend, hrecv, dsend, drecv, esend, erecv, local_sem,
):
    band, row, zlo, core, zhi, x, y = place()
    me = band * 64 + row
    before, after = jnp.minimum(me, 8), jnp.minimum(DEVICES - 1 - me, 8)

    barrier = pltpu.get_barrier_semaphore()

    def greet(where):
        pl.semaphore_signal(barrier, inc=1, device_id=where, device_id_type=MESH)

    for d in range(1, 8):
        greet((band, row - y + (y + d) % 8))
    for d in range(1, 4):
        greet((band, zhi * 32 + ((x + d) % 4) * 8 + y))
    for d in range(1, 16):
        other = (band * 2 + zhi + d) % 16
        greet((other // 2, (other % 2) * 32 + x * 8 + y))
    for d in range(1, 9):
        pl.when(me >= d)(lambda d=d: greet(at_device(me - d)))
        pl.when(me + d < DEVICES)(lambda d=d: greet(at_device(me + d)))

    mine = pl.ds(pl.multiple_of(16 * y, 16), 16)

    @pl.when(core == 0)
    def _():
        for b in range(2):
            wa[b, 4 * zhi + x, mine, 0:INNER] = w_qkv[b, :, 0:INNER]
            mix = w_mix[b].astype(F32)
            wa[b, 4 * zhi + x, mine, INNER : 2 * INNER] = jnp.concatenate(
                [mix[:, :512], mix[:, 512:]], axis=0
            ).astype(BF16)
            wa[b, 4 * zhi + x, mine, 2 * INNER :] = w_head[b]

    @pl.when(core == 1)
    def _():
        for b in range(2):
            wide = w_in[b].astype(F32)
            wb[b, 4 * zhi + x, mine, 0:128] = jnp.concatenate(
                [wide[a : a + 1, 128 * g : 128 * g + 128] for a in range(2) for g in range(8)], axis=0
            ).astype(BF16)
            wb[b, 4 * zhi + x, mine, 128:] = w_qkv[b, :, INNER:]

    halo[8 * TOK :, :] = latent[...].astype(BF16)

    def clear(k, _):
        halo[pl.ds(pl.multiple_of(k * TOK, TOK), TOK), :] = jnp.zeros((TOK, C), BF16)
        return 0

    lax.fori_loop(0, 8 - before, clear, 0)
    column = me // 2
    lower = me % 2

    def clear_column(k, _):
        grid_rows[k] = jnp.zeros((16, 16, C), BF16)
        return 0

    lax.fori_loop(0, jnp.maximum(4 - column, 0), clear_column, 0)

    pl.semaphore_wait(barrier, 25 + before + after)

    sems = dict(
        z=(zsend, zsem),
        ax=(axsend, axsem),
        ay=(aysend, aysem),
        by=(bysend, bysem),
        bx=(bxsend, bxsem),
        side=(side_send, side),
    )
    gather = Gather(wa, wb, sems)
    steps = [list(zip(gather.steps(0, b), gather.steps(1, b))) for b in range(2)]

    def halo_copy(d):
        return pltpu.make_async_remote_copy(
            src_ref=halo.at[pl.ds(8 * TOK, TOK)],
            dst_ref=halo.at[pl.ds((8 - d) * TOK, TOK)],
            send_sem=hsend.at[d],
            recv_sem=hrecv.at[d],
            device_id=at_device(me + d),
            device_id_type=MESH,
        )

    gather.run(steps[0][:2])
    for d in range(1, 9):
        pl.when(me + d < DEVICES)(lambda d=d: halo_copy(d).start())
    gather.run(steps[0][2:])
    gather.run(steps[1])

    for d in range(1, 9):
        pl.when(me >= d)(lambda d=d: halo_copy(d).wait_recv())

    def block(b, window, tokens, chunk, query_rows, key_pos, first_query, first_pos):
        unpack[...] = wb[b, :, :, 0:128].reshape(D, 128).astype(F32)
        for g in range(8):
            win[:, 128 * g : 128 * g + 128] = unpack[pl.ds(g, 128, stride=8), :].astype(BF16)
        packed = wa[b, :, :, INNER : 2 * INNER].reshape(64, 16, 512).astype(F32)
        for part in range(2):
            wmix[:, 512 * part : 512 * part + 512] = packed[:, 8 * part : 8 * part + 8].reshape(512, 512).astype(BF16)

        gain = gain_attn[b : b + 1, :]

        def keys(k, _):
            rows = pl.ds(pl.multiple_of(k * chunk, chunk), chunk)
            hidden = jnp.dot(window(k, chunk), win[...], preferred_element_type=F32)
            normed[0:chunk, :] = (hidden * inverse_rms(hidden) * gain).astype(BF16)
            for part in range(2):
                weights = wb[b, :, :, 128 + 512 * part : 640 + 512 * part].reshape(D, 512)
                pairs[rows, 512 * part : 512 * part + 512] = jnp.dot(
                    normed[0:chunk, :], weights, preferred_element_type=F32
                ).astype(BF16)
            return 0

        lax.fori_loop(0, tokens // chunk, keys, 0)
        hidden = jnp.dot(query_rows, win[...], preferred_element_type=F32)
        queries = jnp.dot(
            (hidden * inverse_rms(hidden) * gain).astype(BF16),
            wa[b, :, :, 0:INNER].reshape(D, INNER),
            preferred_element_type=F32,
        ).astype(BF16)
        query_pos = lax.broadcasted_iota(jnp.int32, (ROWS, 1), 0) + first_query
        allowed = (key_pos <= query_pos) & (key_pos > query_pos - WIN) & (key_pos + first_pos >= 0)
        for head in range(HEADS):
            lanes = slice(HS * head, HS * head + HS)
            scores = lax.dot_general(
                queries[:, lanes], pairs[0:tokens, lanes], (((1,), (1,)), ((), ())), preferred_element_type=F32
            )
            scores = jnp.where(allowed, scores, -1e30)
            weights = jnp.exp2((scores - jnp.max(scores, axis=-1, keepdims=True)) * SCALE)
            total = jnp.sum(weights, axis=-1, keepdims=True)
            values = pairs[0:tokens, INNER + HS * head : INNER + HS * head + HS]
            result = jnp.dot(weights.astype(BF16), values, preferred_element_type=F32)
            attended[:, lanes] = (result / total).astype(BF16)
        hidden = hidden + jnp.dot(attended[...], wmix[...], preferred_element_type=F32)
        params[...] = jnp.dot(
            (hidden * inverse_rms(hidden) * gain_head[b : b + 1, :]).astype(BF16),
            wa[b, :, :, 2 * INNER :].reshape(D, 256),
            preferred_element_type=F32,
        )
        shifted = params[EXTRA - 1 : EXTRA - 1 + TOK, :]
        first = (lax.broadcasted_iota(jnp.int32, (TOK, 1), 0) == 0) & (me == 0)
        return jnp.where(first, 0.0, shifted)

    position = lax.broadcasted_iota(jnp.int32, (1, T0), 1)
    shifted = block(
        0,
        lambda k, n: halo[pl.ds(pl.multiple_of(k * n, n), n), :],
        T0,
        384,
        halo[WIN - EXTRA :, :],
        position,
        WIN - EXTRA,
        me * TOK - WIN,
    )
    state[...] = ((latent[...] - shifted[:, :C]) * jnp.exp(-shifted[:, C:])).astype(BF16)

    source = band * 2 + zhi
    high = y % 2

    def first_stage(g):
        return (high * 2 + g // 4) * 4 + g % 4

    def stage_copy(g):
        target = first_stage(g)
        return pltpu.make_async_remote_copy(
            src_ref=state.at[pl.ds(pl.multiple_of(16 * g, 16), 16)],
            dst_ref=tile_a.at[source],
            send_sem=dsend.at[g],
            recv_sem=drecv,
            device_id=(target // 2, (target % 2) * 32 + x * 8 + y),
            device_id_type=MESH,
        )

    def stage_local(g):
        return pltpu.make_async_copy(
            state.at[pl.ds(pl.multiple_of(16 * g, 16), 16)], tile_a.at[source], local_sem
        )

    for g in range(8):
        mine_too = first_stage(g) == source
        pl.when(mine_too)(lambda g=g: stage_local(g).start())
        pl.when(jnp.logical_not(mine_too))(lambda g=g: stage_copy(g).start())

    relay = zlo // 2 == high
    base = 16 * source
    residue = x * 4 + y // 2
    own_offset = x * 4 + y // 2

    def second_copy(o, half, n, at, slot):
        return pltpu.make_async_remote_copy(
            src_ref=tile_b.at[pl.ds(at, n)],
            dst_ref=grid_rows.at[pl.ds(slot, n), residue],
            send_sem=esend.at[2 * o + half],
            recv_sem=erecv,
            device_id=at_device(2 * (base + o) + half),
            device_id_type=MESH,
        )

    def second_local(o, n, at, slot):
        return pltpu.make_async_copy(tile_b.at[pl.ds(at, n)], grid_rows.at[pl.ds(slot, n), residue], erecv)

    def second_each(act, act_local):
        for o in range(20):
            at, slot = max(o - 4, 0), max(4 - o, 0)
            n = min(o, 15) - at + 1
            for half in range(2):
                if o < 16:
                    ours = (own_offset == o) & (y % 2 == half)
                    if act_local is not None:
                        pl.when(ours)(lambda: act_local(second_local(o, n, at, slot)))
                    pl.when(jnp.logical_not(ours))(lambda: act(second_copy(o, half, n, at, slot)))
                else:
                    pl.when(base + o < G)(lambda: act(second_copy(o, half, n, at, slot)))

    @pl.when(relay)
    def _():
        for g in range(8):
            pl.when(first_stage(g) == source)(lambda g=g: stage_local(g).wait())

        pltpu.make_async_remote_copy(
            src_ref=tile_a.at[pl.ds(0, 15)],
            dst_ref=tile_a.at[pl.ds(0, 15)],
            send_sem=dsend.at[0],
            recv_sem=drecv,
            device_id=(band, row),
            device_id_type=MESH,
        ).wait_recv()
        unpack[0:256, :] = tile_a[...].reshape(256, C).astype(F32)
        for c in range(16):
            tile_b[c] = unpack[pl.ds(c, 16, stride=16), :].astype(BF16)
        second_each(lambda copy: copy.start(), lambda copy: copy.start())

    def slots_got(n):
        pltpu.make_async_remote_copy(
            src_ref=grid_rows.at[pl.ds(5 - n, n)],
            dst_ref=grid_rows.at[pl.ds(5 - n, n)],
            send_sem=esend.at[0],
            recv_sem=erecv,
            device_id=(band, row),
            device_id_type=MESH,
        ).wait_recv()

    for n in range(1, 6):
        pl.when(column + 1 == n if n < 5 else column >= 4)(lambda n=n: slots_got(n))

    unpack[0:256, :] = grid_rows[3].reshape(256, C).astype(F32)
    natural[0:16, :] = unpack[pl.ds(15, 16, stride=16), :]
    unpack[0:256, :] = grid_rows[4].reshape(256, C).astype(F32)
    for m in range(16):
        natural[16 + 16 * m : 32 + 16 * m, :] = unpack[pl.ds(m, 16, stride=16), :]
    query_state[...] = natural[pl.ds(pl.multiple_of(lower * TOK, TOK), ROWS), :]

    place_in = lax.broadcasted_iota(jnp.int32, (1, T1), 1)
    position = place_in // 256 * 256 + place_in % 16 * 16 + place_in // 16 % 16
    shifted = block(
        1,
        lambda k, n: grid_rows[k].reshape(256, C),
        T1,
        256,
        query_state[...].astype(BF16),
        position,
        WIN - EXTRA + lower * TOK,
        (column - 4) * G,
    )
    out[...] = (query_state[EXTRA:, :] - shifted[:, :C]) * jnp.exp(-shifted[:, C:])

    gather.finish()
    for d in range(1, 9):
        pl.when(me + d < DEVICES)(lambda d=d: halo_copy(d).wait_send())
    for g in range(8):
        pl.when(first_stage(g) != source)(lambda g=g: stage_copy(g).wait_send())

    @pl.when(relay)
    def _():
        second_each(lambda copy: copy.wait_send(), None)


def shards(*args):
    vmem = pl.BlockSpec(memory_space=pltpu.VMEM)
    dma = pltpu.SemaphoreType.DMA
    return pl.pallas_call(
        kernel,
        out_shape=jax.ShapeDtypeStruct((TOK, C), F32),
        in_specs=[vmem] * 7,
        out_specs=vmem,
        scratch_shapes=[
            pltpu.VMEM((2, 8, 128, NA), BF16),
            pltpu.VMEM((2, 8, 128, NB), BF16),
            pltpu.VMEM((C, D), BF16),
            pltpu.VMEM((INNER, D), BF16),
            pltpu.VMEM((D, 128), F32),
            pltpu.VMEM((9 * TOK, C), BF16),
            pltpu.VMEM((16, 16, C), BF16),
            pltpu.VMEM((16, 16, C), BF16),
            pltpu.VMEM((5, 16, 16, C), BF16),
            pltpu.VMEM((17 * 16, C), F32),
            pltpu.VMEM((ROWS, C), F32),
            pltpu.VMEM((384, D), BF16),
            pltpu.VMEM((T1, 2 * INNER), BF16),
            pltpu.VMEM((ROWS, INNER), BF16),
            pltpu.VMEM((ROWS, 256), F32),
            pltpu.VMEM((TOK, C), BF16),
            *[dma(shape) for shape in ((2,), (2, 2, 4), (2, 2, 2, 5), (2, 2, 8), (2, 2, 4), (2, 2)) for _ in range(2)],
            dma((9,)),
            dma((9,)),
            dma((8,)),
            dma(()),
            dma((40,)),
            dma(()),
            dma(()),
        ],
        compiler_params=pltpu.CompilerParams(collective_id=0, has_side_effects=True, vmem_limit_bytes=56 << 20),
    )(*args)


def solution(mesh):
    return jax.shard_map(
        shards,
        mesh=mesh,
        in_specs=(
            P(("band", "row"), None),
            P(None, "row", None),
            P(None, "row", None),
            P(None, "row", None),
            P(None, "row", None),
            P(),
            P(),
        ),
        out_specs=P(("band", "row"), None),
        check_vma=False,
    )
```

time: 1190 us -> 122 us (0.10)
  blocking collectives: 850 us -> 0 us
  waiting for transfers between devices: 181 us -> 0 us
  Pallas kernels: 0 us -> 120 us
  starting transfers between devices: 92.5 us -> 0 us
  matrix products: 26 us -> 0 us
  between operations: 13.8 us -> 0.01 us
  local copies, waits for them, and re-layouts: 13.6 us -> 1.47 us
    all_gather x4 -> x0, blocking collectives: 784 us -> none  [the longest x2 402 us: flow_block(): hidden = contract(rounded, lax.all_gather(w_in, 'row', axis=0, tiled=True))]
    ppermute x18 -> x0, waiting for transfers between devices: 180 us -> none  [passed_along(): return lax.ppermute(x, axis, pairs)]
    pallas_call x0 -> x1, Pallas kernels: none -> 120 us  [shards(): pl.pallas_call(kernel, out_shape=jax.ShapeDtypeStruct((TOK, C), F32), in_...]
    ppermute x18 -> x0, starting transfers between devices: 85.2 us -> none  [passed_along(): return lax.ppermute(x, axis, pairs)]
    all_to_all x1 -> x0, blocking collectives: 65.8 us -> none  [transpose_grid(): lax.all_to_all(outgoing.astype(jnp.bfloat16), 'band', split_axis=0, conca...]
    dot_general x12 -> x0, matrix products: 18.6 us -> none  [the longest x6 5.34 us: contract(): return jnp.dot(left, shard_rows, preferred_element_type=jnp.float32)]
  transfers between devices with their start and end apart: 23 -> 0, of which waited for: 11 -> 0; matrix products, arithmetic and copies ran while one was open for 3% -> 0% of each run, Pallas kernels for 0% -> 0%
where the time goes in v1:
time: 122 us
  Pallas kernels  120 us (98%)
  local copies, waits for them, and re-layouts  1.47 us (1%)
    pallas_call x1, Pallas kernels, shards(): pl.pallas_call(kernel, out_shape=jax.ShapeDtypeStruct((TOK, C), F32), in_...  120 us

profile of v1, /device:TPU:1, one launch (start us, length us, event | category | flops | bytes accessed | tf_op | source)
XLA Modules:
  0.0 121.5 jit_solution(18249468114875800101)
XLA Ops:
  0.0 120.1 %shard_map.73 = f32[128,128]{1,0:T(8,128)} custom-call(f32[128,128]{1,0:T(8,128)} %latent.1, bf16[2,2,1024]{2,1,0:T(2,128)(2,1)} %w_in.1, bf16[2,16,1536]{2,1,0:T(8,128)(2,1)} %w_qkv.1, bf16[2,8,1024]{2,1,0:T(8,128)(2,1)} %w_mix.1, bf16[2,16,256]{2,1,0:T(8,128)(2,1)} %w_head.1, f32[2,1024]{1,0:T(2,128)} %gain_attn.1, f32[2,1024]{1,0:T(2,128)} %gain_head.1), custom_call_target="tpu_custom_call" | custom-call | tf_op jit(solution)/shard_map/pallas_call | solution.py:462
  120.1 1.5 %copy.9 = f32[128,128]{1,0:T(8,128)} copy(f32[128,128]{1,0:T(8,128)} %shard_map.73) | data formatting | bytes 131072

commit v2 on v1

--- a/solution.py
+++ b/solution.py
@@ -20,6 +20,7 @@
 T0 = WIN + TOK
 T1 = 5 * G
 EPS = 1e-06
+HOOKS = (2, 3, 3, 4, 4, 5, 6)
 SCALE = math.log2(math.e) / math.sqrt(HS)
 
 
@@ -180,11 +181,11 @@
     wa, wb, win, wmix, unpack, halo, tile_a, tile_b, grid_rows, natural, query_state,
     normed, pairs, attended, params, state,
     zsem, zsend, axsem, axsend, aysem, aysend, bysem, bysend, bxsem, bxsend, side, side_send,
-    hsend, hrecv, dsend, drecv, esend, erecv, local_sem,
+    hsend, hrecv, dsend, drecv, esend, erecv, local_sem, ready,
 ):
     band, row, zlo, core, zhi, x, y = place()
     me = band * 64 + row
-    before, after = jnp.minimum(me, 8), jnp.minimum(DEVICES - 1 - me, 8)
+    before = jnp.minimum(me, 8)
 
     barrier = pltpu.get_barrier_semaphore()
 
@@ -195,12 +196,14 @@
         greet((band, row - y + (y + d) % 8))
     for d in range(1, 4):
         greet((band, zhi * 32 + ((x + d) % 4) * 8 + y))
-    for d in range(1, 16):
-        other = (band * 2 + zhi + d) % 16
-        greet((other // 2, (other % 2) * 32 + x * 8 + y))
-    for d in range(1, 9):
-        pl.when(me >= d)(lambda d=d: greet(at_device(me - d)))
-        pl.when(me + d < DEVICES)(lambda d=d: greet(at_device(me + d)))
+    for d in range(1, 4):
+        greet((((zlo + d) % 4) * 2 + core, row))
+    greet((band, (row + 32) % 64))
+    greet((zlo * 2 + 1 - core, row))
+    tail = row >= 56
+    upper, under = tail & (core == 1) & (zlo < 3), tail & (core == 0) & (zlo > 0)
+    pl.when(upper)(lambda: greet((band + 1, row)))
+    pl.when(under)(lambda: greet((band - 1, row)))
 
     mine = pl.ds(pl.multiple_of(16 * y, 16), 16)
 
@@ -239,7 +242,7 @@
 
     lax.fori_loop(0, jnp.maximum(4 - column, 0), clear_column, 0)
 
-    pl.semaphore_wait(barrier, 25 + before + after)
+    pl.semaphore_wait(barrier, 15 + (upper | under).astype(jnp.int32))
 
     sems = dict(
         z=(zsend, zsem),
@@ -262,16 +265,28 @@
             device_id_type=MESH,
         )
 
-    gather.run(steps[0][:2])
+    gather.run(steps[0][:5])
     for d in range(1, 9):
-        pl.when(me + d < DEVICES)(lambda d=d: halo_copy(d).start())
-    gather.run(steps[0][2:])
-    gather.run(steps[1])
-
+        pl.when(row + d < 64)(lambda d=d: halo_copy(d).start())
+
+    @pl.when(tail & (band > 0))
+    def _():
+        pl.semaphore_signal(ready, inc=1, device_id=(band - 1, row), device_id_type=MESH)
+
+    gather.run(steps[0][5:6])
+
+    @pl.when(tail & (band < 7))
+    def _():
+        pl.semaphore_wait(ready, 1)
+        for d in range(1, 9):
+            pl.when(row + d >= 64)(lambda d=d: halo_copy(d).start())
+
+    gather.run(steps[0][6:])
+    gather.run(steps[1][:2])
     for d in range(1, 9):
         pl.when(me >= d)(lambda d=d: halo_copy(d).wait_recv())
 
-    def block(b, window, tokens, chunk, query_rows, key_pos, first_query, first_pos):
+    def block(b, window, tokens, chunk, query_rows, key_pos, first_query, first_pos, between):
         unpack[...] = wb[b, :, :, 0:128].reshape(D, 128).astype(F32)
         for g in range(8):
             win[:, 128 * g : 128 * g + 128] = unpack[pl.ds(g, 128, stride=8), :].astype(BF16)
@@ -293,6 +308,7 @@
             return 0
 
         lax.fori_loop(0, tokens // chunk, keys, 0)
+        between(0)
         hidden = jnp.dot(query_rows, win[...], preferred_element_type=F32)
         queries = jnp.dot(
             (hidden * inverse_rms(hidden) * gain).astype(BF16),
@@ -312,6 +328,7 @@
             values = pairs[0:tokens, INNER + HS * head : INNER + HS * head + HS]
             result = jnp.dot(weights.astype(BF16), values, preferred_element_type=F32)
             attended[:, lanes] = (result / total).astype(BF16)
+            between(head + 1)
         hidden = hidden + jnp.dot(attended[...], wmix[...], preferred_element_type=F32)
         params[...] = jnp.dot(
             (hidden * inverse_rms(hidden) * gain_head[b : b + 1, :]).astype(BF16),
@@ -332,6 +349,7 @@
         position,
         WIN - EXTRA,
         me * TOK - WIN,
+        lambda k: gather.run(steps[1][HOOKS[k] : HOOKS[k + 1]]),
     )
     state[...] = ((latent[...] - shifted[:, :C]) * jnp.exp(-shifted[:, C:])).astype(BF16)
 
@@ -362,6 +380,7 @@
         pl.when(mine_too)(lambda g=g: stage_local(g).start())
         pl.when(jnp.logical_not(mine_too))(lambda g=g: stage_copy(g).start())
 
+    gather.run(steps[1][HOOKS[5] : HOOKS[6]])
     relay = zlo // 2 == high
     base = 16 * source
     residue = x * 4 + y // 2
@@ -411,6 +430,8 @@
             tile_b[c] = unpack[pl.ds(c, 16, stride=16), :].astype(BF16)
         second_each(lambda copy: copy.start(), lambda copy: copy.start())
 
+    gather.run(steps[1][HOOKS[6] :])
+
     def slots_got(n):
         pltpu.make_async_remote_copy(
             src_ref=grid_rows.at[pl.ds(5 - n, n)],
@@ -442,6 +463,7 @@
         position,
         WIN - EXTRA + lower * TOK,
         (column - 4) * G,
+        lambda k: None,
     )
     out[...] = (query_state[EXTRA:, :] - shifted[:, :C]) * jnp.exp(-shifted[:, C:])
 
@@ -489,6 +511,7 @@
             dma((40,)),
             dma(()),
             dma(()),
+            pltpu.SemaphoreType.REGULAR,
         ],
         compiler_params=pltpu.CompilerParams(collective_id=0, has_side_effects=True, vmem_limit_bytes=56 << 20),
     )(*args)

time: 122 us -> 101 us (0.83)
  Pallas kernels: 120 us -> 99.7 us
    pallas_call x1, Pallas kernels: 120 us -> 99.7 us  [shards(): pl.pallas_call(kernel, out_shape=jax.ShapeDtypeStruct((TOK, C), F32), in_...]
where the time goes in v2:
time: 101 us
  Pallas kernels  99.7 us (99%)
  local copies, waits for them, and re-layouts  1.47 us (1%)
    pallas_call x1, Pallas kernels, shards(): pl.pallas_call(kernel, out_shape=jax.ShapeDtypeStruct((TOK, C), F32), in_...  99.7 us

profile of v2, /device:TPU:1, one launch (start us, length us, event | category | flops | bytes accessed | tf_op | source)
XLA Modules:
  0.0 101.2 jit_solution(4636172169216042939)
XLA Ops:
  0.0 99.7 %shard_map.73 = f32[128,128]{1,0:T(8,128)} custom-call(f32[128,128]{1,0:T(8,128)} %latent.1, bf16[2,2,1024]{2,1,0:T(2,128)(2,1)} %w_in.1, bf16[2,16,1536]{2,1,0:T(8,128)(2,1)} %w_qkv.1, bf16[2,8,1024]{2,1,0:T(8,128)(2,1)} %w_mix.1, bf16[2,16,256]{2,1,0:T(8,128)(2,1)} %w_head.1, f32[2,1024]{1,0:T(2,128)} %gain_attn.1, f32[2,1024]{1,0:T(2,128)} %gain_head.1), custom_call_target="tpu_custom_call" | custom-call | tf_op jit(solution)/shard_map/pallas_call | solution.py:484
  99.7 1.5 %copy.9 = f32[128,128]{1,0:T(8,128)} copy(f32[128,128]{1,0:T(8,128)} %shard_map.73) | data formatting | bytes 131072

commit v3 on v2

--- a/solution.py
+++ b/solution.py
@@ -37,6 +37,7 @@
     def __init__(self, wa, wb, sems):
         self.wa, self.wb, self.s = wa, wb, sems
         self.band, self.row, self.zlo, self.core, self.zhi, self.x, self.y = place()
+        self.z = self.zhi * 4 + self.zlo
         self.sent = ({}, {})
 
     def at(self, x=None, y=None, zhi=None, core=None):
@@ -48,6 +49,8 @@
 
     def copy(self, ref, sem, where):
         name, *index = sem
+        if name == "az":
+            index[1] = self.half(index[1])
         return pltpu.make_async_remote_copy(
             src_ref=ref,
             dst_ref=ref,
@@ -71,8 +74,8 @@
     def cell(self, w, b, h, x, y):
         return w.at[b, 4 * self.half(h) + x, pl.ds(pl.multiple_of(16 * y, 16), 16)]
 
-    def column(self, w, b, h, y):
-        return w.at[b, pl.ds(4 * self.half(h), 4), pl.ds(pl.multiple_of(16 * y, 16), 16)]
+    def column(self, w, b, h, y, part):
+        return w.at[b, pl.ds(4 * self.half(h) + 2 * part, 2), pl.ds(pl.multiple_of(16 * y, 16), 16)]
 
     def line(self, w, b, h, x):
         return w.at[b, 4 * self.half(h) + x]
@@ -89,25 +92,42 @@
         for d in (1, 3, 2):
             self.send(0, self.cell(self.wa, b, h, self.x, self.y), ("ax", b, h, d), self.at(x=(self.x + d) % 4))
 
-    def a_side(self, b, h, y):
-        self.send(0, self.column(self.wa, b, h, y), ("side", b, h), self.at(core=1))
+    def a_side(self, b, h, y, part):
+        self.send(0, self.column(self.wa, b, h, y, part), ("side", b, h), self.at(core=1))
 
     def a_y(self, b, h, k):
-        last = (4, 3) if h == 0 else (3, 4)
+        part = self.z % 2
         if k == 0:
             for d in (1, 3, 2):
                 self.got(self.cell(self.wa, b, h, (self.x - d) % 4, self.y), ("ax", b, h, d))
-        for way, step in ((0, 1), (1, -1)):
-            if k > last[way]:
-                continue
-            y = (self.y - step * k) % 8
-            ref = self.column(self.wa, b, h, y)
-            if k > 0:
-                self.got(ref, ("ay", b, h, way, k))
-            if k < last[way]:
-                self.send(0, ref, ("ay", b, h, way, k + 1), self.at(y=(self.y + step) % 8))
-            if k > 0 or way == 0:
-                self.a_side(b, h, y)
+            for d in (2, 6, 1, 7):
+                self.a_on(b, h, 0, d)
+            self.a_side(b, h, self.y, 0)
+            self.a_side(b, h, self.y, 1)
+        for d in ((), (2, 6, 1, 7), (3, 5, 4))[k]:
+            y = (self.y - d) % 8
+            ref = self.column(self.wa, b, h, y, part)
+            self.got(ref, ("ay", b, h, d))
+            if d == 2:
+                self.a_on(b, h, 2, 1)
+            if d == 6:
+                self.a_on(b, h, 6, 7)
+            if d == 2 + 4 * h:
+                self.a_on(b, h, d, d)
+            z = (self.z + 1 - 2 * self.half(h)) % 8
+            self.send(0, ref, ("az", b, h, 8 - d), ((z % 4) * 2 + self.core, (z // 4) * 32 + self.x * 8 + self.y))
+            self.a_side(b, h, y, part)
+
+    def a_on(self, b, h, came, d):
+        ref = self.column(self.wa, b, h, (self.y - came) % 8, self.z % 2)
+        self.send(0, ref, ("ay", b, h, (came + d) % 8), self.at(y=(self.y + d) % 8))
+
+    def a_z(self, b, h, k):
+        for d in ((), (2, 6, 1, 7), (3, 5, 4))[k]:
+            y = (self.y + d) % 8
+            ref = self.column(self.wa, b, h, y, 1 - self.z % 2)
+            self.got(ref, ("az", b, h, d))
+            self.a_side(b, h, y, 1 - self.z % 2)
 
     def b_y(self, b, h):
         for d in (4, 3, 5, 2, 6, 1, 7):
@@ -116,7 +136,7 @@
     def b_x(self, b, h):
         for d in range(1, 8):
             self.got(self.cell(self.wb, b, h, self.x, (self.y - d) % 8), ("by", b, h, d))
-        for d in (2, 1, 3):
+        for d in (1, 3):
             self.send(1, self.line(self.wb, b, h, self.x), ("bx", b, h, d), self.at(x=(self.x + d) % 4))
         self.b_side(b, h, self.x)
 
@@ -126,6 +146,8 @@
     def b_on(self, b, h, d):
         x = (self.x - d) % 4
         self.got(self.line(self.wb, b, h, x), ("bx", b, h, d))
+        if d == 1 + 2 * h:
+            self.send(1, self.line(self.wb, b, h, x), ("bx", b, h, 2), self.at(x=(self.x + 2 - d) % 4))
         self.b_side(b, h, x)
 
     def side_got(self, core, b):
@@ -138,18 +160,28 @@
             yield lambda: self.across(0, b)
             yield lambda: self.a_x(b, 0)
             yield lambda: (self.across_got(0, b), self.a_x(b, 1))
-            for k in range(5):
-                yield lambda k=k: (self.a_y(b, 0, k), self.a_y(b, 1, k))
+            yield lambda: (self.a_y(b, 0, 0), None)
+            yield lambda: (self.a_y(b, 1, 0), None)
+            yield lambda: (self.a_y(b, 0, 1), self.a_y(b, 1, 1))
+            yield lambda: (self.a_z(b, 0, 1), self.a_z(b, 1, 1))
+            yield lambda: (self.a_y(b, 0, 2), self.a_y(b, 1, 2))
+            yield lambda: (self.a_z(b, 0, 2), self.a_z(b, 1, 2))
         else:
             yield lambda: self.across(1, b)
             yield lambda: self.b_y(b, 0)
             yield lambda: (self.across_got(1, b), self.b_y(b, 1))
             yield lambda: self.b_x(b, 0)
             yield lambda: self.b_x(b, 1)
-            yield lambda: (self.b_on(b, 0, 1), self.b_on(b, 0, 3), self.b_on(b, 0, 2))
-            yield lambda: (self.b_on(b, 1, 1), self.b_on(b, 1, 3), self.b_on(b, 1, 2))
+            yield lambda: (self.b_on(b, 0, 1), self.b_on(b, 0, 3))
+            yield lambda: (self.b_on(b, 1, 3), self.b_on(b, 1, 1), self.b_on(b, 0, 2), self.b_on(b, 1, 2))
             yield lambda: None
-        yield lambda: self.side_got(core, b)
+            yield lambda: None
+
+    def early(self, b):
+        pl.when(self.core == 0)(lambda: self.side_got(0, b))
+
+    def late(self, b):
+        pl.when(self.core == 1)(lambda: self.side_got(1, b))
 
     def run(self, pairs):
         for first, second in pairs:
@@ -164,7 +196,7 @@
                 w = (self.wa, self.wb)[core]
                 whole = dict(
                     cell=w.at[0, 0, pl.ds(0, 16)],
-                    column=w.at[0, pl.ds(0, 4), pl.ds(0, 16)],
+                    column=w.at[0, pl.ds(0, 2), pl.ds(0, 16)],
                     line=w.at[0, 0],
                     half=w.at[0, pl.ds(0, 4)],
                 )
@@ -180,7 +212,7 @@
     latent, w_in, w_qkv, w_mix, w_head, gain_attn, gain_head, out,
     wa, wb, win, wmix, unpack, halo, tile_a, tile_b, grid_rows, natural, query_state,
     normed, pairs, attended, params, state,
-    zsem, zsend, axsem, axsend, aysem, aysend, bysem, bysend, bxsem, bxsend, side, side_send,
+    zsem, zsend, axsem, axsend, aysem, aysend, azsem, azsend, bysem, bysend, bxsem, bxsend, side, side_send,
     hsend, hrecv, dsend, drecv, esend, erecv, local_sem, ready,
 ):
     band, row, zlo, core, zhi, x, y = place()
@@ -200,6 +232,9 @@
         greet((((zlo + d) % 4) * 2 + core, row))
     greet((band, (row + 32) % 64))
     greet((zlo * 2 + 1 - core, row))
+    for d in (1, 7):
+        z = (zhi * 4 + zlo + d) % 8
+        greet(((z % 4) * 2 + core, (z // 4) * 32 + x * 8 + y))
     tail = row >= 56
     upper, under = tail & (core == 1) & (zlo < 3), tail & (core == 0) & (zlo > 0)
     pl.when(upper)(lambda: greet((band + 1, row)))
@@ -242,12 +277,13 @@
 
     lax.fori_loop(0, jnp.maximum(4 - column, 0), clear_column, 0)
 
-    pl.semaphore_wait(barrier, 15 + (upper | under).astype(jnp.int32))
+    pl.semaphore_wait(barrier, 17 + (upper | under).astype(jnp.int32))
 
     sems = dict(
         z=(zsend, zsem),
         ax=(axsend, axsem),
         ay=(aysend, aysem),
+        az=(azsend, azsem),
         by=(bysend, bysem),
         bx=(bxsend, bxsem),
         side=(side_send, side),
@@ -281,8 +317,8 @@
         for d in range(1, 9):
             pl.when(row + d >= 64)(lambda d=d: halo_copy(d).start())
 
-    gather.run(steps[0][6:])
-    gather.run(steps[1][:2])
+    gather.run(steps[0][6:7])
+    gather.early(0)
     for d in range(1, 9):
         pl.when(me >= d)(lambda d=d: halo_copy(d).wait_recv())
 
@@ -290,10 +326,6 @@
         unpack[...] = wb[b, :, :, 0:128].reshape(D, 128).astype(F32)
         for g in range(8):
             win[:, 128 * g : 128 * g + 128] = unpack[pl.ds(g, 128, stride=8), :].astype(BF16)
-        packed = wa[b, :, :, INNER : 2 * INNER].reshape(64, 16, 512).astype(F32)
-        for part in range(2):
-            wmix[:, 512 * part : 512 * part + 512] = packed[:, 8 * part : 8 * part + 8].reshape(512, 512).astype(BF16)
-
         gain = gain_attn[b : b + 1, :]
 
         def keys(k, _):
@@ -307,8 +339,13 @@
                 ).astype(BF16)
             return 0
 
-        lax.fori_loop(0, tokens // chunk, keys, 0)
+        lax.fori_loop(0, tokens // chunk - 1, keys, 0)
+        between(-1)
+        lax.fori_loop(tokens // chunk - 1, tokens // chunk, keys, 0)
         between(0)
+        packed = wa[b, :, :, INNER : 2 * INNER].reshape(64, 16, 512).astype(F32)
+        for part in range(2):
+            wmix[:, 512 * part : 512 * part + 512] = packed[:, 8 * part : 8 * part + 8].reshape(512, 512).astype(BF16)
         hidden = jnp.dot(query_rows, win[...], preferred_element_type=F32)
         queries = jnp.dot(
             (hidden * inverse_rms(hidden) * gain).astype(BF16),
@@ -339,6 +376,16 @@
         first = (lax.broadcasted_iota(jnp.int32, (TOK, 1), 0) == 0) & (me == 0)
         return jnp.where(first, 0.0, shifted)
 
+    def in_block(k):
+        if k < 0:
+            gather.run(steps[0][7:8])
+            gather.run(steps[1][: HOOKS[0]])
+            return
+        if k == 0:
+            gather.run(steps[0][8:])
+            gather.late(0)
+        gather.run(steps[1][HOOKS[k] : HOOKS[k + 1]])
+
     position = lax.broadcasted_iota(jnp.int32, (1, T0), 1)
     shifted = block(
         0,
@@ -349,7 +396,7 @@
         position,
         WIN - EXTRA,
         me * TOK - WIN,
-        lambda k: gather.run(steps[1][HOOKS[k] : HOOKS[k + 1]]),
+        in_block,
     )
     state[...] = ((latent[...] - shifted[:, :C]) * jnp.exp(-shifted[:, C:])).astype(BF16)
 
@@ -431,6 +478,7 @@
         second_each(lambda copy: copy.start(), lambda copy: copy.start())
 
     gather.run(steps[1][HOOKS[6] :])
+    gather.early(1)
 
     def slots_got(n):
         pltpu.make_async_remote_copy(
@@ -463,7 +511,7 @@
         position,
         WIN - EXTRA + lower * TOK,
         (column - 4) * G,
-        lambda k: None,
+        lambda k: gather.late(1) if k == 0 else None,
     )
     out[...] = (query_state[EXTRA:, :] - shifted[:, :C]) * jnp.exp(-shifted[:, C:])
 
@@ -503,7 +551,7 @@
             pltpu.VMEM((ROWS, INNER), BF16),
             pltpu.VMEM((ROWS, 256), F32),
             pltpu.VMEM((TOK, C), BF16),
-            *[dma(shape) for shape in ((2,), (2, 2, 4), (2, 2, 2, 5), (2, 2, 8), (2, 2, 4), (2, 2)) for _ in range(2)],
+            *[dma(shape) for shape in ((2,), (2, 2, 4), (2, 2, 8), (2, 2, 8), (2, 2, 8), (2, 2, 4), (2, 2)) for _ in range(2)],
             dma((9,)),
             dma((9,)),
             dma((8,)),

time: 101 us -> 97.5 us (0.965)
  Pallas kernels: 99.7 us -> 95.8 us
    pallas_call x1, Pallas kernels: 99.7 us -> 95.8 us  [shards(): pl.pallas_call(kernel, out_shape=jax.ShapeDtypeStruct((TOK, C), F32), in_...]
where the time goes in v3:
time: 97.5 us; the launch traced here: 97.3 us
  Pallas kernels  95.8 us (98%)
  local copies, waits for them, and re-layouts  1.47 us (2%)
    pallas_call x1, Pallas kernels, shards(): pl.pallas_call(kernel, out_shape=jax.ShapeDtypeStruct((TOK, C), F32), in_...  95.8 us

profile of v3, /device:TPU:1, one launch (start us, length us, event | category | flops | bytes accessed | tf_op | source)
XLA Modules:
  0.0 97.3 jit_solution(3597086488873823136)
XLA Ops:
  0.0 95.8 %shard_map.73 = f32[128,128]{1,0:T(8,128)} custom-call(f32[128,128]{1,0:T(8,128)} %latent.1, bf16[2,2,1024]{2,1,0:T(2,128)(2,1)} %w_in.1, bf16[2,16,1536]{2,1,0:T(8,128)(2,1)} %w_qkv.1, bf16[2,8,1024]{2,1,0:T(8,128)(2,1)} %w_mix.1, bf16[2,16,256]{2,1,0:T(8,128)(2,1)} %w_head.1, f32[2,1024]{1,0:T(2,128)} %gain_attn.1, f32[2,1024]{1,0:T(2,128)} %gain_head.1), custom_call_target="tpu_custom_call" | custom-call | tf_op jit(solution)/shard_map/pallas_call | solution.py:532
  95.8 1.5 %copy.9 = f32[128,128]{1,0:T(8,128)} copy(f32[128,128]{1,0:T(8,128)} %shard_map.73) | data formatting | bytes 131072
